TPU v7x, 32 devices: a whole 2x2x4 slice. The times are simulated.
32 devices in a mesh: dp: 8 (over z, x), tensor: 4 (over y, core).
Axes of the slice: x: 2, y: 2, z: 4, core: 2. Of those that a mesh axis runs over, the one named last changes fastest.
Arguments:
- activations: bfloat16 [4096, 5120], P('dp', 'tensor'), may hold values from -6 to 6
- out_grad: bfloat16 [4096, 5120], P('dp', 'tensor'), may hold values from -6 to 6
- gate_pre: bfloat16 [4096, 14336], P('dp', 'tensor'), may hold values from -6 to 6
- up_pre: bfloat16 [4096, 14336], P('dp', 'tensor'), may hold values from -6 to 6
- down_weight: bfloat16 [14336, 5120], P(('tensor', 'dp')), may hold values from -0.046875 to 0.046875
- proj_model: bfloat16 [5120, 64], replicated, may hold values from -0.078125 to 0.078125
- proj_hidden: bfloat16 [14336, 64], P('tensor'), may hold values from -0.046875 to 0.046875
- lengths: int32 [32], P('dp'), may hold values from 1 to 128, as said below
Outputs:
- grad_gate: bfloat16 [4096, 14336], P('dp', 'tensor')
- grad_up: bfloat16 [4096, 14336], P('dp', 'tensor')
- features: float32 [32, 3, 4096], P('dp')
Inputs may be any that keep to these rules, and one draw needn't show every extreme that they name: In every block of 4 slots of one index of dp the lengths sum to at most 512. In every draw one slot among all 32 has exactly 128 tokens and another exactly 1.
All inputs are finite; a program needn't handle non-finite values.
Results may differ from a plain program's by a relative error of at most 0.003.
Values may be sent and summed in bfloat16 or wider, within the bound.
A program may use at most 128 MiB of HBM per device.

v0:
```python
import jax
import jax.numpy as jnp
from jax import lax
from jax.sharding import PartitionSpec as P


def pair_features(weight, left, right):
    rows, slots = weight.shape
    width = left.shape[1]
    spread = (weight[:, :, None] * left[:, None, :]).reshape(rows, slots * width)
    mats = lax.dot_general(
        spread,
        right,
        (((0,), (0,)), ((), ())),
        precision=lax.Precision.HIGHEST,
        preferred_element_type=jnp.float32,
    )
    return mats.reshape(slots, width * width)


def on_device(
    activations, out_grad, gate_pre, up_pre, down_weight, proj_model, proj_hidden, lengths
):
    rows_here = activations.shape[0]
    offsets = jnp.cumsum(lengths) - lengths
    rows = jnp.arange(rows_here, dtype=jnp.int32)[:, None]
    member = jnp.logical_and(rows >= offsets[None, :], rows < (offsets + lengths)[None, :]).astype(
        jnp.float32
    )
    live = jnp.sum(member, axis=1)
    masked_part = out_grad * live[:, None].astype(jnp.bfloat16)
    masked = lax.all_gather(masked_part, "tensor", axis=1, tiled=True)
    full_rows = lax.all_gather(down_weight, "dp", axis=0, tiled=True)
    hidden_grad = lax.dot_general(
        masked, full_rows, (((1,), (1,)), ((), ())), preferred_element_type=jnp.float32
    )
    gate32 = gate_pre.astype(jnp.float32)
    up32 = up_pre.astype(jnp.float32)
    sig = jax.nn.sigmoid(gate32)
    silu = gate32 * sig
    grad_up = (hidden_grad * silu).astype(jnp.bfloat16)
    grad_gate = (hidden_grad * up32 * sig * (1.0 + gate32 * (1.0 - sig))).astype(jnp.bfloat16)
    hidden = (silu * up32).astype(jnp.bfloat16)
    hidden_part = jnp.dot(hidden, proj_hidden, preferred_element_type=jnp.float32)
    gate_part = jnp.dot(grad_gate, proj_hidden, preferred_element_type=jnp.float32)
    up_part = jnp.dot(grad_up, proj_hidden, preferred_element_type=jnp.float32)
    width = proj_hidden.shape[1]
    whole_inputs = lax.all_gather(activations, "tensor", axis=1, tiled=True)
    in_proj = jnp.dot(whole_inputs, proj_model, preferred_element_type=jnp.float32)
    summed = lax.psum(jnp.concatenate([hidden_part, gate_part, up_part], axis=1), "tensor")
    hidden_proj = summed[:, :width]
    gate_proj = summed[:, width : 2 * width]
    up_proj = summed[:, 2 * width :]
    out_proj = jnp.dot(masked, proj_model, preferred_element_type=jnp.float32)
    weight = member / jnp.sqrt(lengths.astype(jnp.float32))[None, :]
    features = jnp.stack(
        [
            pair_features(weight, in_proj, gate_proj),
            pair_features(weight, in_proj, up_proj),
            pair_features(weight, hidden_proj, out_proj),
        ],
        axis=1,
    )
    return (grad_gate, grad_up, features)


def solution(mesh):
    return jax.shard_map(
        on_device,
        mesh=mesh,
        in_specs=(
            P("dp", "tensor"),
            P("dp", "tensor"),
            P("dp", "tensor"),
            P("dp", "tensor"),
            P(("tensor", "dp"), None),
            P(),
            P("tensor", None),
            P("dp"),
        ),
        out_specs=(P("dp", "tensor"), P("dp", "tensor"), P("dp", None, None)),
        check_vma=False,
    )
```

profile of v0, /device:TPU:0, one launch (start us, length us, event | category | flops | bytes accessed | tf_op | source)
XLA Modules:
  0.0 842.7 jit_solution(14690642394956606823)
XLA Ops:
  7.2 0.0 all-gather.4.cloned.1.call-start
  7.2 0.8 convert_sqrt_fusion
  8.0 0.8 reduce-window.8
  8.8 0.7 bitcast_subtract_fusion
  9.5 0.1 convert_divide_fusion
  9.6 2.5 broadcast_multiply_fusion
  12.1 0.0 all-gather.4.cloned.1.call-update
  12.1 0.0 all-gather.6.cloned.1.call-start
  12.2 0.7 all-gather.6.cloned.1.call-update
  12.9 0.0 all-gather.8.cloned.1.call-start
  12.9 0.7 all-gather.8.cloned.1.call-update
  13.6 0.0 all-reduce.2.cloned.1.call-start
  13.7 4.6 fusion.8
  18.2 37.2 %all-gather.4.cloned.1.call-done = bf16[512,5120]{1,0:T(8,128)(2,1)} async-done(((bf16[512,1280]{1,0:T(8,128)(2,1)}), bf16[512,5120]{1,0:T(8,128)(2,1)}) %all-gather.4.cloned.1.call-update) | async-done | bytes 5242896 | tf_op jit(solution)/shard_map/all_gather | solution.py:32
  55.4 4.0 fusion.19
  59.4 694.3 %all-gather.6.cloned.1.call-done = bf16[3584,5120]{1,0:T(8,128)(2,1)} async-done(((bf16[448,5120]{1,0:T(8,128)(2,1)}), bf16[3584,5120]{1,0:T(8,128)(2,1)}) %all-gather.6.cloned.1.call-update) | async-done | bytes 36700176 | tf_op jit(solution)/shard_map/all_gather | solution.py:33
  753.7 31.8 %multiply_convert_fusion = (bf16[512,3584]{1,0:T(8,128)(2,1)}, bf16[512,3584]{1,0:T(8,128)(2,1)}) fusion(bf16[512,3584]{1,0:T(8,128)(2,1)} %param.10, bf16[512,3584]{1,0:T(8,128)(2,1)} %param.11, bf16[512,5120]{1,0:T(8,128)(2,1)} %all-gather.4.cloned.1.call-done, bf16[3584,5120]{1,0:T(8,128)(2,1)} %all-gather.6.cloned.1.call-done), kind=kOutput, calls=%fused_computation.13 | convolution fusion | flops 18818007040 | bytes 56623104 | tf_op jit(solution)/shard_map/dot_general | solution.py:34
  785.5 3.2 fusion.17
  788.7 3.3 fusion.18
  792.0 0.8 pad_maximum_fusion
  792.8 2.9 all-gather.8.cloned.1.call-done
  795.7 4.2 fusion.16
  799.9 30.6 %all-reduce.2.cloned.1.call-done = f32[512,192]{0,1:T(8,128)} async-done(((f32[512,192]{0,1:T(8,128)}), f32[512,192]{0,1:T(8,128)}) %all-reduce.2.cloned.1.call-update) | async-done | bytes 393232 | tf_op jit(solution)/shard_map/psum | solution.py:50
  830.5 0.9 slice.14
  831.5 0.1 broadcast_multiply_fusion.2
  831.6 1.5 fusion.12
  833.1 0.1 stack_reshape.9
  833.2 1.5 fusion.10
  834.6 0.1 stack_reshape.10
  834.8 0.6 fusion.20
  835.3 0.1 stack_reshape.11
  835.5 0.7 pad_maximum_fusion.1
  (5 shorter events, 0.0 us)
Async XLA Ops:
  7.2 48.3 %copy-start = (bf16[5120,64]{0,1:T(8,128)(2,1)S(1)}, bf16[5120,64]{0,1:T(8,128)(2,1)}, u32[]{:S(2)}) copy-start(bf16[5120,64]{0,1:T(8,128)(2,1)} %param.13) | copy-start | bytes 1966084
  7.2 6.5 copy-start.1
  7.2 48.2 %all-gather.4.cloned.1.call-start = ((), (), s32[]{:S(2)}) async-start(), calls=%async_computation | async-start | bytes 6553600 | tf_op jit(solution)/shard_map/all_gather | solution.py:32
  12.1 741.6 %all-gather.6.cloned.1.call-start = ((), (), s32[]{:S(2)}) async-start(), calls=%async_computation.1 | async-start | bytes 41287680 | tf_op jit(solution)/shard_map/all_gather | solution.py:33
  12.9 782.8 %all-gather.8.cloned.1.call-start = ((), (), s32[]{:S(2)}) async-start(), calls=%async_computation.2 | async-start | bytes 6553600 | tf_op jit(solution)/shard_map/all_gather | solution.py:48
  13.6 816.9 %all-reduce.2.cloned.1.call-start = ((), (), s32[]{:S(2)}) async-start(), calls=%async_computation.3 | async-start | bytes 786432 | tf_op jit(solution)/shard_map/psum | solution.py:50
Sparse Core Ops, SparseCore 0:
  12.3 43.1 all-gather.3
  57.0 696.6 all-gather.5
  755.3 40.4 all-gather.7
  797.9 32.5 all-reduce.1
where the time goes:
time: 843 us
  waiting for transfers between devices  766 us (91%)
  matrix products  54.5 us (6%)
  between operations  13.8 us (2%)
    all_gather x1, waiting for transfers between devices, on_device(): full_rows = lax.all_gather(down_weight, 'dp', axis=0, tiled=True)  694 us
    all_gather x1, waiting for transfers between devices, on_device(): masked = lax.all_gather(masked_part, 'tensor', axis=1, tiled=True)  37.2 us
    dot_general x1, matrix products, on_device(): lax.dot_general(masked, full_rows, (((1,), (1,)), ((), ())), preferred_el...  31.8 us
    psum x1, waiting for transfers between devices, on_device(): lax.psum(jnp.concatenate([hidden_part, gate_part, up_part], axis=1), 'ten...  30.6 us
  transfers between devices with their start and end apart: 4, of which 4 were waited for; matrix products, arithmetic and copies ran while one was open for 6% of the time, Pallas kernels for 0%

commit v1 on v0

v1 whole, which is shorter than its diff:
```python
import functools

import jax
import jax.numpy as jnp
from jax import lax
from jax.experimental import pallas as pl
from jax.experimental.pallas import tpu as pltpu
from jax.sharding import PartitionSpec as P

MESH = pl.DeviceIdType.MESH
LEVELS = 32767.0


def plan(mesh):
    n_dp, n_tensor = mesh.shape["dp"], mesh.shape["tensor"]
    nz = 4 if n_dp % 4 == 0 else n_dp
    nc = 2 if n_tensor % 2 == 0 else 1
    return nz, n_dp // nz, n_tensor // nc, nc


def grad_kernel(
    nz, nx, ny, nc, tok_in, w_in, q_out, sc_out,
    tok, w, qs, scs,
    loc, zs, zr, ys, yr, cs, cr, xs, xr, rs, rr, ss, sr,
):
    dp = lax.axis_index("dp")
    tn = lax.axis_index("tensor")
    z, x = lax.div(dp, nx), lax.rem(dp, nx)
    y, c = lax.div(tn, nc), lax.rem(tn, nc)
    width = tok.shape[3]
    n_t = ny * nc

    def at_z(zz):
        return (zz * nx + x, tn)

    def at_x(k):
        return (z * nx + lax.rem(x + k, nx), tn)

    def at_y(k):
        return (dp, lax.rem(y + k, ny) * nc + c)

    def at_c(k):
        return (dp, y * nc + lax.rem(c + k, nc))

    barrier = pltpu.get_barrier_semaphore()
    peers = [at_z(lax.rem(z + k, nz)) for k in range(1, nz)]
    peers += [at_x(k) for k in range(1, nx)]
    peers += [at_y(k) for k in range(1, ny)]
    peers += [at_c(k) for k in range(1, nc)]
    own_tok = pltpu.make_async_copy(tok_in, tok.at[z, tn], loc.at[0])
    own_tok.start()
    own_w = pltpu.make_async_copy(w_in, w.at[x], loc.at[1])
    own_w.start()
    for peer in peers:
        pl.semaphore_signal(barrier, inc=1, device_id=peer, device_id_type=MESH)
    pl.semaphore_wait(barrier, len(peers))

    def remote(src, dst, send, recv, device):
        return pltpu.make_async_remote_copy(
            src_ref=src, dst_ref=dst, send_sem=send, recv_sem=recv,
            device_id=device, device_id_type=MESH,
        )

    def w_copy(k):
        return remote(w_in, w.at[x], xs.at[k - 1], xr.at[x], at_x(k))

    def z_copy(b, side):
        target = z + 1 if side else z - 1
        return remote(tok.at[b, tn], tok.at[b, tn], zs.at[b, side], zr.at[b], at_z(target))

    def y_copy(b, k):
        return remote(tok.at[b, tn], tok.at[b, tn], ys.at[b, k - 1], yr.at[b, k - 1], at_y(k))

    def c_copy(b, k, kc):
        t = lax.rem(y - k + ny, ny) * nc + c
        return remote(tok.at[b, t], tok.at[b, t], cs.at[b, k, kc - 1], cr.at[b, k, kc - 1], at_c(kc))

    def q_copy(b, xi):
        return remote(qs.at[b, xi], q_out.at[z, xi], rs.at[b, xi], rr.at[z, xi], at_z(b))

    def sc_copy(b, xi):
        return remote(scs.at[b, xi], sc_out.at[z, xi], ss.at[b, xi], sr.at[z, xi], at_z(b))

    def q_own(xi):
        return pltpu.make_async_copy(qs.at[z, xi], q_out.at[z, xi], rs.at[z, xi])

    def sc_own(xi):
        return pltpu.make_async_copy(scs.at[z, xi], sc_out.at[z, xi], ss.at[z, xi])

    near = jnp.minimum(z, nz - 1 - z)

    def block_of(i):
        half = lax.div(i + 1, 2)
        both = jnp.where(lax.rem(i, 2) == 1, z - half, z + half)
        tail = jnp.where(z == near, i, nz - 1 - i)
        return jnp.where(i <= 2 * near, both, tail)

    def goes_right(b):
        return jnp.logical_and(b <= z, z < nz - 1)

    def goes_left(b):
        return jnp.logical_and(b >= z, z > 0)

    def spread(b):
        pl.when(goes_right(b))(lambda: z_copy(b, 1).start())
        pl.when(goes_left(b))(lambda: z_copy(b, 0).start())
        for k in range(1, ny):
            y_copy(b, k).start()
        for kc in range(1, nc):
            c_copy(b, 0, kc).start()

    def complete(b):
        for k in range(1, ny):
            y_copy(b, k).wait_recv()
            for kc in range(1, nc):
                c_copy(b, k, kc).start()
        for k in range(ny):
            for kc in range(1, nc):
                c_copy(b, k, kc).wait_recv()

    def product(b, xi):
        total = None
        for t in range(n_t):
            part = lax.dot_general(
                tok[b, t], w[xi, :, t * width:(t + 1) * width],
                (((1,), (1,)), ((), ())), preferred_element_type=jnp.float32,
            )
            total = part if total is None else total + part
        top = jnp.maximum(jnp.max(jnp.abs(total), axis=0, keepdims=True), 1e-30)
        qs[b, xi] = jnp.round(total * (LEVELS / top)).astype(jnp.int32).astype(jnp.int16)
        scs[b, xi] = jnp.broadcast_to(top * (1.0 / LEVELS), scs.shape[2:])

        @pl.when(b == z)
        def _():
            q_own(xi).start()
            sc_own(xi).start()

        @pl.when(b != z)
        def _():
            q_copy(b, xi).start()
            sc_copy(b, xi).start()

    own_tok.wait()
    spread(z)
    for k in range(1, nx):
        w_copy(k).start()
    own_w.wait()

    @pl.loop(1, nz + 1)
    def _(i):
        @pl.when(i < nz)
        def _():
            b = block_of(i)
            z_copy(b, 0).wait_recv()
            spread(b)

        b = block_of(i - 1)
        complete(b)
        product(b, x)

    for k in range(1, nx):
        xi = lax.rem(x - k + nx, nx)
        remote(w_in, w.at[xi], xs.at[k - 1], xr.at[xi], at_x(k)).wait_recv()

        @pl.loop(0, nz)
        def _(i):
            product(block_of(lax.rem(i + 1, nz)), xi)

    for k in range(1, nx):
        w_copy(k).wait_send()

    @pl.loop(0, nz)
    def _(b):
        pl.when(goes_right(b))(lambda: z_copy(b, 1).wait_send())
        pl.when(goes_left(b))(lambda: z_copy(b, 0).wait_send())
        for k in range(1, ny):
            y_copy(b, k).wait_send()
        for k in range(ny):
            for kc in range(1, nc):
                c_copy(b, k, kc).wait_send()
        for xi in range(nx):
            @pl.when(b == z)
            def _():
                q_own(xi).wait()
                sc_own(xi).wait()

            @pl.when(b != z)
            def _():
                q_copy(b, xi).wait_send()
                sc_copy(b, xi).wait_send()
                remote(qs.at[b, xi], q_out.at[b, xi], rs.at[b, xi], rr.at[b, xi], at_z(b)).wait_recv()
                remote(scs.at[b, xi], sc_out.at[b, xi], ss.at[b, xi], sr.at[b, xi], at_z(b)).wait_recv()


def hidden_grads(sizes, masked_part, down_weight):
    nz, nx, ny, nc = sizes
    rows, width = masked_part.shape
    units, model = down_weight.shape
    n_t = ny * nc
    dma = pltpu.SemaphoreType.DMA
    any_spec = pl.BlockSpec(memory_space=pl.ANY)
    return pl.pallas_call(
        functools.partial(grad_kernel, nz, nx, ny, nc),
        out_shape=(
            jax.ShapeDtypeStruct((nz, nx, rows, units), jnp.int16),
            jax.ShapeDtypeStruct((nz, nx, 8, units), jnp.float32),
        ),
        in_specs=[any_spec, any_spec],
        out_specs=(any_spec, any_spec),
        scratch_shapes=[
            pltpu.VMEM((nz, n_t, rows, width), jnp.bfloat16),
            pltpu.VMEM((nx, units, model), jnp.bfloat16),
            pltpu.VMEM((nz, nx, rows, units), jnp.int16),
            pltpu.VMEM((nz, nx, 8, units), jnp.float32),
            dma((2,)),
            dma((nz, 2)), dma((nz,)),
            dma((nz, max(ny - 1, 1))), dma((nz, max(ny - 1, 1))),
            dma((nz, ny, max(nc - 1, 1))), dma((nz, ny, max(nc - 1, 1))),
            dma((max(nx - 1, 1),)), dma((nx,)),
            dma((nz, nx)), dma((nz, nx)),
            dma((nz, nx)), dma((nz, nx)),
        ],
        compiler_params=pltpu.CompilerParams(
            collective_id=0, has_side_effects=True, vmem_limit_bytes=56 * 2**20
        ),
        cost_estimate=pl.CostEstimate(
            flops=2 * nz * rows * nx * units * model,
            bytes_accessed=2 * (rows * width + units * model + nz * nx * rows * units),
            transcendentals=0,
        ),
        name="hidden_grads",
    )(masked_part, down_weight)


def epilogue_kernel(nz, nx, q_ref, sc_ref, gate_ref, up_ref, proj_ref, gg_ref, gu_ref, part_ref):
    rows = gate_ref.shape[0]
    units = q_ref.shape[3]
    chunk = nx * units
    total = None
    for zz in range(nz):
        cols = slice(zz * chunk, (zz + 1) * chunk)
        grad = jnp.concatenate(
            [
                q_ref[zz, xi].astype(jnp.int32).astype(jnp.float32) * sc_ref[zz, xi, 0:1, :]
                for xi in range(nx)
            ],
            axis=1,
        )
        gate32 = gate_ref[:, cols].astype(jnp.float32)
        up32 = up_ref[:, cols].astype(jnp.float32)
        sig = jax.nn.sigmoid(gate32)
        silu = gate32 * sig
        gu = (grad * silu).astype(jnp.bfloat16)
        gg = (grad * up32 * sig * (1.0 + gate32 * (1.0 - sig))).astype(jnp.bfloat16)
        hid = (silu * up32).astype(jnp.bfloat16)
        gu_ref[:, cols] = gu
        gg_ref[:, cols] = gg
        stacked = jnp.concatenate([gg, gu, hid], axis=0)
        part = jnp.dot(stacked, proj_ref[cols, :], preferred_element_type=jnp.float32)
        total = part if total is None else total + part
    for i in range(3):
        part_ref[i] = total[i * rows:(i + 1) * rows]


def epilogue(sizes, q, sc, gate_pre, up_pre, proj_hidden):
    nz, nx = sizes[:2]
    rows, hidden = gate_pre.shape
    units, rank = q.shape[3], proj_hidden.shape[1]
    tile = 128
    row_spec = pl.BlockSpec((tile, hidden), lambda i: (i, 0))
    return pl.pallas_call(
        functools.partial(epilogue_kernel, nz, nx),
        grid=(rows // tile,),
        in_specs=[
            pl.BlockSpec((nz, nx, tile, units), lambda i: (0, 0, i, 0)),
            pl.BlockSpec((nz, nx, 8, units), lambda i: (0, 0, 0, 0)),
            row_spec,
            row_spec,
            pl.BlockSpec((hidden, rank), lambda i: (0, 0)),
        ],
        out_specs=(row_spec, row_spec, pl.BlockSpec((3, tile, rank), lambda i: (0, i, 0))),
        out_shape=(
            jax.ShapeDtypeStruct((rows, hidden), jnp.bfloat16),
            jax.ShapeDtypeStruct((rows, hidden), jnp.bfloat16),
            jax.ShapeDtypeStruct((3, rows, rank), jnp.float32),
        ),
        compiler_params=pltpu.CompilerParams(vmem_limit_bytes=48 * 2**20),
        name="epilogue",
    )(q, sc, gate_pre, up_pre, proj_hidden)


def pair_features(weight, left, right):
    rows, slots = weight.shape
    width = left.shape[1]
    spread = (weight[:, :, None] * left[:, None, :]).reshape(rows, slots * width)
    mats = lax.dot_general(
        spread,
        right,
        (((0,), (0,)), ((), ())),
        precision=lax.Precision.HIGHEST,
        preferred_element_type=jnp.float32,
    )
    return mats.reshape(slots, width * width)


def on_device(
    sizes, activations, out_grad, gate_pre, up_pre, down_weight, proj_model, proj_hidden, lengths
):
    rows_here, width_here = activations.shape
    offsets = jnp.cumsum(lengths) - lengths
    rows = jnp.arange(rows_here, dtype=jnp.int32)[:, None]
    member = jnp.logical_and(rows >= offsets[None, :], rows < (offsets + lengths)[None, :]).astype(
        jnp.float32
    )
    live = jnp.sum(member, axis=1)
    masked_part = out_grad * live[:, None].astype(jnp.bfloat16)
    proj_here = lax.dynamic_slice_in_dim(
        proj_model, lax.axis_index("tensor") * width_here, width_here, axis=0
    )
    early = jnp.concatenate(
        [
            jnp.dot(activations, proj_here, preferred_element_type=jnp.float32),
            jnp.dot(masked_part, proj_here, preferred_element_type=jnp.float32),
        ],
        axis=1,
    )
    early = lax.psum(early, "tensor")
    q, sc = hidden_grads(sizes, masked_part, down_weight)
    grad_gate, grad_up, parts = epilogue(sizes, q, sc, gate_pre, up_pre, proj_hidden)
    rank = proj_hidden.shape[1]
    in_proj, out_proj = early[:, :rank], early[:, rank:]
    weight = member / jnp.sqrt(lengths.astype(jnp.float32))[None, :]
    features = jnp.stack(
        [
            pair_features(weight, in_proj, parts[0]),
            pair_features(weight, in_proj, parts[1]),
            pair_features(weight, parts[2], out_proj),
        ],
        axis=1,
    )
    return (grad_gate, grad_up, lax.psum(features, "tensor"))


def solution(mesh):
    return jax.shard_map(
        functools.partial(on_device, plan(mesh)),
        mesh=mesh,
        in_specs=(
            P("dp", "tensor"),
            P("dp", "tensor"),
            P("dp", "tensor"),
            P("dp", "tensor"),
            P(("tensor", "dp"), None),
            P(),
            P("tensor", None),
            P("dp"),
        ),
        out_specs=(P("dp", "tensor"), P("dp", "tensor"), P("dp", None, None)),
        check_vma=False,
    )
```

time: 843 us -> 272 us (0.32)
  waiting for transfers between devices: 766 us -> 34.7 us
  Pallas kernels: 0 us -> 210 us
  matrix products: 54.5 us -> 2.76 us
    all_gather x3 -> x0, waiting for transfers between devices: 734 us -> none  [the longest x1 694 us: on_device(): full_rows = lax.all_gather(down_weight, 'dp', axis=0, tiled=True)]
    pallas_call x0 -> x2, Pallas kernels: none -> 210 us  [the longest x1 200 us: hidden_grads(): pl.pallas_call(functools.partial(grad_kernel, nz, nx, ny, nc), out_shape=...]
    dot_general x6 -> x2, matrix products: 51 us -> 1.02 us  [the longest x1 0.52 us: on_device(): jnp.dot(activations, proj_here, preferred_element_type=jnp.float32)]
    psum x1 -> x2, waiting for transfers between devices: 30.6 us -> 34.7 us  [the longest x1 34.7 us: on_device(): return (grad_gate, grad_up, lax.psum(features, 'tensor'))]
  transfers between devices with their start and end apart: 4 -> 2, of which waited for: 4 -> 1; matrix products, arithmetic and copies ran while one was open for 6% -> 0% of each run, Pallas kernels for 0% -> 77%
where the time goes in v1:
time: 272 us; the launch traced here: 271 us
  Pallas kernels  210 us (77%)
  waiting for transfers between devices  34.7 us (13%)
  between operations  14.2 us (5%)
  other arithmetic  5.45 us (2%)
  local copies, waits for them, and re-layouts  4.34 us (2%)
  matrix products  2.76 us (1%)
    pallas_call x1, Pallas kernels, hidden_grads(): pl.pallas_call(functools.partial(grad_kernel, nz, nx, ny, nc), out_shape=...  200 us
    psum x1, waiting for transfers between devices, on_device(): return (grad_gate, grad_up, lax.psum(features, 'tensor'))  34.7 us
    pallas_call x1, Pallas kernels, epilogue(): pl.pallas_call(functools.partial(epilogue_kernel, nz, nx), grid=(rows //...  9.42 us
  transfers between devices with their start and end apart: 2, of which 1 were waited for; matrix products, arithmetic and copies ran while one was open for 0% of the time, Pallas kernels for 77%

profile of v1, /device:TPU:0, one launch (start us, length us, event | category | flops | bytes accessed | tf_op | source)
XLA Modules:
  0.0 271.2 jit_solution(6934369775138452938)
XLA Ops:
  7.2 0.0 copy-start
  7.2 0.0 all-reduce.3.cloned.1.call-start
  7.2 0.8 convert_sqrt_fusion
  8.0 0.8 reduce-window.8
  8.8 0.7 bitcast_subtract_fusion
  9.5 0.1 convert_divide_fusion
  9.6 1.5 broadcast_multiply_fusion.tok_in
  11.1 0.0 copy-start.3
  11.1 0.5 convolution_bitcast_fusion
  11.7 0.5 fusion.6
  12.2 0.0 copy-done.3
  12.2 0.7 pad_maximum_fusion
  12.9 0.0 all-reduce.3.cloned.1.call-update
  13.0 0.0 all-reduce.5.cloned.1.call-start
  13.0 0.4 copy.13.proj_ref
  13.5 200.2 %hidden_grads.1 = (s16[4,2,512,448]{3,2,1,0:T(8,128)(2,1)}, f32[4,2,8,448]{3,2,1,0:T(8,128)}) custom-call(bf16[512,1280]{1,0:T(8,128)(2,1)} %copy-done.3, bf16[448,5120]{1,0:T(8,128)(2,1)} %w_in.1), custom_call_target="tpu_custom_call" | custom-call | flops 18790481920 | bytes 9568256 | tf_op jit(solution)/shard_map/hidden_grads/pallas_call | solution.py:202
  213.7 0.9 copy-done.2
  214.6 9.4 %epilogue.1 = (bf16[512,3584]{1,0:T(8,128)(2,1)}, bf16[512,3584]{1,0:T(8,128)(2,1)}, f32[3,512,64]{2,1,0:T(8,128)S(1)}) custom-call(s16[4,2,512,448]{3,2,1,0:T(8,128)(2,1)} %get-tuple-element.8.q_ref, f32[4,2,8,448]{3,2,1,0:T(8,128)S(1)} %copy-done.2, bf16[512,3584]{1,0:T(8,128)(2,1)S(1)} %copy-done.1, bf16[512,3584]{1,0:T(8,128)(2,1)} %up_ref.1, ...), custom_call_target="tpu_custom_call" | custom-call | tf_op jit(solution)/shard_map/epilogue/pallas_call | solution.py:271
  224.0 0.1 copy.16
  224.1 0.0 all-reduce.3.cloned.1.call-done
  224.2 0.9 slice.20
  225.1 0.1 broadcast_multiply_fusion.2
  225.2 0.6 fusion
  225.8 0.6 fusion.2
  226.4 0.6 fusion.9
  227.0 0.1 stack_reshape.11
  227.1 0.1 stack_reshape.9
  227.2 0.1 stack_reshape.10
  227.3 0.7 pad_maximum_fusion.1
  228.0 0.0 all-reduce.5.cloned.1.call-update
  228.1 34.7 %all-reduce.5.cloned.1.call-done = f32[4,3,4096]{2,0,1:T(4,128)} async-done(((f32[4,3,4096]{2,0,1:T(4,128)}), f32[4,3,4096]{2,0,1:T(4,128)}) %all-reduce.5.cloned.1.call-update) | async-done | bytes 196624 | tf_op jit(solution)/shard_map/psum | solution.py:341
  262.7 1.6 copy.23
  (11 shorter events, 0.0 us)
Async XLA Ops:
  7.2 4.0 %copy-start = (bf16[512,1280]{1,0:T(8,128)(2,1)S(1)}, bf16[512,1280]{1,0:T(8,128)(2,1)}, u32[]{:S(2)}) copy-start(bf16[512,1280]{1,0:T(8,128)(2,1)} %param.8) | copy-start | bytes 3932164
  7.2 217.0 %all-reduce.3.cloned.1.call-start = ((), (), s32[]{:S(2)}) async-start(), calls=%async_computation | async-start | bytes 524288 | tf_op jit(solution)/shard_map/psum | solution.py:327
  9.6 1.6 copy-start.6
  11.1 1.1 copy-start.3
  11.7 1.4 copy-start.4
  13.0 249.8 %all-reduce.5.cloned.1.call-start = ((), (), s32[]{:S(2)}) async-start(), calls=%async_computation.1 | async-start | bytes 393216 | tf_op jit(solution)/shard_map/psum | solution.py:341
  13.5 200.2 %copy-start.1 = (bf16[512,3584]{1,0:T(8,128)(2,1)S(1)}, bf16[512,3584]{1,0:T(8,128)(2,1)}, u32[]{:S(2)}) copy-start(bf16[512,3584]{1,0:T(8,128)(2,1)} %gate_ref.1) | copy-start | bytes 11010052
  213.7 0.9 copy-start.2
  225.1 1.3 copy-start.5
Sparse Core Ops, SparseCore 0:
  13.1 36.6 all-reduce.2
  228.2 34.4 all-reduce.4

commit v2 on v1

--- a/solution.py
+++ b/solution.py
@@ -303,6 +303,17 @@
     return mats.reshape(slots, width * width)
 
 
+def sum_over_tensor(value, n_tensor):
+    if n_tensor & (n_tensor - 1):
+        return lax.psum(value, "tensor")
+    step = 1
+    while step < n_tensor:
+        pairs = [(i, i ^ step) for i in range(n_tensor)]
+        value = value + lax.ppermute(value, "tensor", pairs)
+        step *= 2
+    return value
+
+
 def on_device(
     sizes, activations, out_grad, gate_pre, up_pre, down_weight, proj_model, proj_hidden, lengths
 ):
@@ -338,7 +349,7 @@
         ],
         axis=1,
     )
-    return (grad_gate, grad_up, lax.psum(features, "tensor"))
+    return (grad_gate, grad_up, sum_over_tensor(features, sizes[2] * sizes[3]))
 
 
 def solution(mesh):

time: 272 us -> 245 us (0.901)
  waiting for transfers between devices: 34.7 us -> 7.77 us
    psum x1 -> x0, waiting for transfers between devices: 34.7 us -> none  [on_device(): return (grad_gate, grad_up, lax.psum(features, 'tensor'))]
    ppermute x0 -> x2, waiting for transfers between devices: none -> 7.73 us  [sum_over_tensor(): value = value + lax.ppermute(value, 'tensor', pairs)]
  transfers between devices with their start and end apart: 2 -> 3, of which waited for: 1 -> 2; matrix products, arithmetic and copies ran while one was open for 0% -> 0% of each run, Pallas kernels for 77% -> 86%
where the time goes in v2:
time: 245 us; the launch traced here: 244 us
  Pallas kernels  210 us (86%)
  between operations  14.2 us (6%)
  waiting for transfers between devices  7.77 us (3%)
  other arithmetic  5.5 us (2%)
  matrix products  2.77 us (1%)
  local copies, waits for them, and re-layouts  2.76 us (1%)
    pallas_call x1, Pallas kernels, hidden_grads(): pl.pallas_call(functools.partial(grad_kernel, nz, nx, ny, nc), out_shape=...  200 us
    pallas_call x1, Pallas kernels, epilogue(): pl.pallas_call(functools.partial(epilogue_kernel, nz, nx), grid=(rows //...  9.41 us
    ppermute x2, waiting for transfers between devices, sum_over_tensor(): value = value + lax.ppermute(value, 'tensor', pairs)  7.73 us
  transfers between devices with their start and end apart: 3, of which 2 were waited for; matrix products, arithmetic and copies ran while one was open for 0% of the time, Pallas kernels for 86%

profile of v2, /device:TPU:0, one launch (start us, length us, event | category | flops | bytes accessed | tf_op | source)
XLA Modules:
  0.0 243.8 jit_solution(11320750704552830850)
XLA Ops:
  7.2 0.0 copy-start
  7.2 0.0 all-reduce.2.cloned.1.call-start
  7.2 0.8 convert_sqrt_fusion
  8.0 0.8 reduce-window.8
  8.8 0.7 bitcast_subtract_fusion
  9.5 0.1 convert_divide_fusion
  9.6 1.5 broadcast_multiply_fusion.tok_in
  11.1 0.0 copy-start.3
  11.1 0.5 convolution_bitcast_fusion
  11.7 0.5 fusion.6
  12.2 0.7 pad_maximum_fusion
  12.9 0.0 all-reduce.2.cloned.1.call-update
  13.0 0.4 copy.13.proj_ref
  13.4 200.2 %hidden_grads.1 = (s16[4,2,512,448]{3,2,1,0:T(8,128)(2,1)}, f32[4,2,8,448]{3,2,1,0:T(8,128)}) custom-call(bf16[512,1280]{1,0:T(8,128)(2,1)} %copy-done.3, bf16[448,5120]{1,0:T(8,128)(2,1)} %w_in.1), custom_call_target="tpu_custom_call" | custom-call | flops 18790481920 | bytes 9568256 | tf_op jit(solution)/shard_map/hidden_grads/pallas_call | solution.py:202
  213.6 0.9 copy-done.2
  214.5 9.4 %epilogue.1 = (bf16[512,3584]{1,0:T(8,128)(2,1)}, bf16[512,3584]{1,0:T(8,128)(2,1)}, f32[3,512,64]{2,1,0:T(8,128)S(1)}) custom-call(s16[4,2,512,448]{3,2,1,0:T(8,128)(2,1)} %get-tuple-element.8.q_ref, f32[4,2,8,448]{3,2,1,0:T(8,128)S(1)} %copy-done.2, bf16[512,3584]{1,0:T(8,128)(2,1)S(1)} %copy-done.1, bf16[512,3584]{1,0:T(8,128)(2,1)} %up_ref.1, ...), custom_call_target="tpu_custom_call" | custom-call | tf_op jit(solution)/shard_map/epilogue/pallas_call | solution.py:271
  224.0 0.1 copy.16
  224.1 0.0 all-reduce.2.cloned.1.call-done
  224.1 0.9 slice.20
  225.0 0.1 broadcast_multiply_fusion.1
  225.2 0.6 fusion
  225.8 0.6 fusion.2
  226.4 0.6 fusion.9
  226.9 0.1 stack_reshape.11
  227.0 0.1 stack_reshape.9
  227.1 0.1 stack_reshape.10
  227.3 0.6 collective-permute-start
  227.9 1.1 collective-permute-done
  228.9 0.1 add.13
  229.0 0.6 collective-permute-start.1
  229.6 6.7 %collective-permute-done.1 = f32[4,3,4096]{2,0,1:T(4,128)S(1)} collective-permute-done((f32[4,3,4096]{2,0,1:T(4,128)S(1)}, f32[4,3,4096]{2,0,1:T(4,128)S(1)}, u32[]{:S(2)}, u32[]{:S(2)}) %collective-permute-start.1) | collective-permute-done | bytes 196640 | tf_op jit(solution)/shard_map/ppermute | solution.py:312
  236.2 0.7 add.14
  (15 shorter events, 0.1 us)
Async XLA Ops:
  7.2 4.0 %copy-start = (bf16[512,1280]{1,0:T(8,128)(2,1)S(1)}, bf16[512,1280]{1,0:T(8,128)(2,1)}, u32[]{:S(2)}) copy-start(bf16[512,1280]{1,0:T(8,128)(2,1)} %param.8) | copy-start | bytes 3932164
  7.2 216.9 %all-reduce.2.cloned.1.call-start = ((), (), s32[]{:S(2)}) async-start(), calls=%async_computation | async-start | bytes 524288 | tf_op jit(solution)/shard_map/psum | solution.py:338
  9.6 1.6 copy-start.6
  11.1 1.1 copy-start.3
  11.7 1.3 copy-start.4
  13.4 200.2 %copy-start.1 = (bf16[512,3584]{1,0:T(8,128)(2,1)S(1)}, bf16[512,3584]{1,0:T(8,128)(2,1)}, u32[]{:S(2)}) copy-start(bf16[512,3584]{1,0:T(8,128)(2,1)} %gate_ref.1) | copy-start | bytes 11010052
  213.6 0.9 copy-start.2
  225.0 1.3 copy-start.5
  227.3 1.6 collective-permute-start
  229.0 7.2 %collective-permute-start.1 = (f32[4,3,4096]{2,0,1:T(4,128)S(1)}, f32[4,3,4096]{2,0,1:T(4,128)S(1)}, u32[]{:S(2)}, u32[]{:S(2)}) collective-permute-start(f32[4,3,4096]{2,0,1:T(4,128)S(1)} %add.13), channel_id=1, source_target_pairs={{0,2},{1,3},{2,0},{3,1},{4,6},{5,7},{6,4},{7,5},{8,10},{9,11},{10,... | collective-permute-start | bytes 589832 | tf_op jit(solution)/shard_map/ppermute | solution.py:312
Sparse Core Ops, SparseCore 0:
  13.1 36.6 all-reduce.1
